TPU v7x, 32 devices: a whole 2x2x4 slice. The times are simulated.
32 devices in a mesh: sess: 8 (over z, core), tp: 4 (over y, x).
Axes of the slice: x: 2, y: 2, z: 4, core: 2. Of those that a mesh axis runs over, the one named last changes fastest.
Arguments:
- frames: bfloat16 [128, 4096], P('sess', 'tp'), may hold values from -6 to 6
- norm_gain: bfloat16 [4096], replicated, may hold values from 0.5 to 1.5
- w_qkv: bfloat16 [3, 4096, 2048], P(None, None, 'tp'), may hold values from -0.09375 to 0.09375
- w_out: bfloat16 [2048, 4096], P('tp'), may hold values from -0.5 to 0.5
- kv_cache: bfloat16 [2, 256, 375, 2048], P(None, 'sess', None, 'tp'), may hold values from -800 to 800
- frame_session: int32 [128], replicated, may hold values from 0 to 127, as said below
- owner_of: int32 [128], replicated, may hold values from 0 to 7, as said below
- context_len: int32 [128], replicated, may hold values from 1 to 375, as said below
Outputs:
- hidden_rows: bfloat16 [128, 4096], P('sess', 'tp')
Inputs may be any that keep to these rules, and one draw needn't show every extreme that they name: `frame_session`: a permutation of the sessions; at most 4 of the frame rows of one index of sess have the same owner, and some rows reach 4. `owner_of`: each owner holds at most 32 sessions, and some owner holds exactly 32. `context_len`: some session has exactly 375.
All inputs are finite; a program needn't handle non-finite values.
Results may differ from a plain program's by a relative error of at most 0.014.
The roundings to bfloat16 on the way count: a program that leaves them out, or rounds other values in their place, can miss the bound.
Values may be sent and summed in bfloat16 or wider, within the bound.
A program may use at most 128 MiB of HBM per device.

v0:
```python
import functools

import jax
import jax.numpy as jnp
from jax import lax
from jax.experimental import pallas as pl
from jax.experimental.pallas import tpu as pltpu
from jax.sharding import PartitionSpec as P

HD = 128
LANES = 128
MESH = pl.DeviceIdType.MESH
F32 = jnp.float32
BF16 = jnp.bfloat16


def quot(x, k):
    if k & (k - 1) == 0:
        return lax.shift_right_logical(x, jnp.full_like(x, k.bit_length() - 1))
    return lax.div(x, jnp.full_like(x, k))


def rest(x, k):
    return x - quot(x, k) * k


def iota(rows, cols, axis):
    return lax.broadcasted_iota(jnp.int32, (rows, cols), axis)


def one_hot(cond):
    return jnp.where(cond, 1.0, 0.0).astype(BF16)


def routing(me, n, heads, cap, msg, rows, slots, sessions, fs, owner, length):
    def pick(cond, values, axis):
        return jnp.sum(jnp.where(cond, values, 0.0), axis=axis, keepdims=True)

    i0, i1 = iota(sessions, sessions, 0), iota(sessions, sessions, 1)
    eye = i0 == i1

    def as_col(row):
        return pick(eye, row, 1)

    owner_c = as_col(owner)
    slot_c = pick((owner_c == owner) & (i1 < i0), 1.0, 1)
    match = i0 == fs
    row_owner = pick(match, owner_c, 0)
    row_slot = pick(match, slot_c, 0)
    row_len = pick(match, as_col(length), 0)
    row_owner_c, row_slot_c = as_col(row_owner), as_col(row_slot)
    block0, block1 = quot(i0, rows), quot(i1, rows)
    row_pair = pick((row_owner_c == row_owner) & (block0 == block1) & (i0 < i1), 1.0, 0)
    target = row_owner * cap + row_pair
    place = quot(iota(1, sessions, 1), rows).astype(F32) * cap + row_pair
    target_c, place_c = as_col(target), as_col(place)
    me_f = me.astype(F32)

    stack, total, held = heads * rows, n * msg, heads * slots

    def message_code(i):
        inner = rest(i, msg)
        return quot(inner, cap), (quot(i, msg) * cap + rest(inner, cap)).astype(F32)

    local = pick(
        iota(sessions, stack, 0) == me * rows + rest(iota(sessions, stack, 1), rows), target_c, 0
    )
    head_i, code = message_code(iota(total, stack, 0))
    send = one_hot((head_i == quot(iota(total, stack, 1), rows)) & (code == local))
    local_c = pick(
        iota(stack, sessions, 1) == me * rows + rest(iota(stack, sessions, 0), rows), target, 1
    )
    head_i, code = message_code(iota(stack, total, 1))
    unsend = one_hot((head_i == quot(iota(stack, total, 0), rows)) & (code == local_c))

    in_slot = (row_slot == rest(iota(held, sessions, 0), slots).astype(F32)) & (row_owner == me_f)
    _, code = message_code(iota(sessions, total, 1))
    spread = jnp.dot(one_hot(in_slot), one_hot(place_c == code), preferred_element_type=F32)
    head_i, _ = message_code(iota(held, total, 1))
    collect = jnp.where(head_i == quot(iota(held, total, 0), slots), spread, 0.0).astype(BF16)
    in_slot_t = (row_slot_c == rest(iota(sessions, held, 1), slots).astype(F32)) & (
        row_owner_c == me_f
    )
    _, code = message_code(iota(total, sessions, 0))
    spread = jnp.dot(one_hot(place == code), one_hot(in_slot_t), preferred_element_type=F32)
    head_i, _ = message_code(iota(total, held, 0))
    uncollect = jnp.where(head_i == quot(iota(total, held, 1), slots), spread, 0.0).astype(BF16)

    held_len = pick(in_slot, row_len, 1)
    lane = iota(held, LANES, 1)
    limit = jnp.where(
        rest(lane, slots) == rest(iota(held, LANES, 0), slots),
        held_len - quot(lane, slots).astype(F32),
        -1.0,
    )
    return send, unsend, collect, uncollect, limit


def kernel(
    dims,
    frames_ref, gain_ref, fs_ref, owner_ref, length_ref, wqkv_hbm, wout_hbm, kv_hbm,
    out_ref,
    w_v, wo_v, kv_v, fr_all, normed, q_send, q_recv, kv_send, kv_recv, r_send, r_recv,
    p_send, p_recv, scores, acc, send_m, unsend_m, collect_m, uncollect_m, limit_m,
    load_sem, ag_s, ag_r, q_s, q_r, kv_s, kv_r, r_s, r_r, p_s, p_r,
):
    n, tp, heads, cap, msg, rows, slots, ctx, tchunk, chunks, kc = dims
    dl = frames_ref.shape[1]
    d_all = dl * tp
    me, mt = lax.axis_index("sess"), lax.axis_index("tp")
    sess_peer = [lax.rem(me + d, n) for d in range(n)]
    tp_peer = [lax.rem(mt + d, tp) for d in range(tp)]

    loads = []

    def load(src, dst):
        loads.append(pltpu.make_async_copy(src, dst, load_sem.at[len(loads)]))
        loads[-1].start()
        return loads[-1]

    w_load = [load(wqkv_hbm.at[c], w_v.at[c]) for c in range(3)]

    barrier = pltpu.get_barrier_semaphore()
    for d in range(1, tp):
        pl.semaphore_signal(barrier, inc=1, device_id=(me, tp_peer[d]), device_id_type=MESH)
    for d in range(1, n):
        pl.semaphore_signal(barrier, inc=1, device_id=(sess_peer[d], mt), device_id_type=MESH)
    pl.semaphore_wait(barrier, n + tp - 2)

    def over_tp(src, dst, s, r, d):
        copy = pltpu.make_async_remote_copy(
            src_ref=src, dst_ref=dst, send_sem=s.at[d - 1], recv_sem=r.at[d - 1],
            device_id=(me, tp_peer[d]), device_id_type=MESH,
        )
        copy.start()
        return copy

    def over_sess(send, recv, s, r):
        copies = []
        for d in range(1, n):
            copy = pltpu.make_async_remote_copy(
                src_ref=send.at[sess_peer[d]], dst_ref=recv.at[me],
                send_sem=s.at[d - 1], recv_sem=r.at[d - 1],
                device_id=(sess_peer[d], mt), device_id_type=MESH,
            )
            copy.start()
            copies.append(copy)
        return copies

    ag = [over_tp(frames_ref, fr_all.at[mt], ag_s, ag_r, d) for d in range(1, tp)]
    kv_load = []
    for c in range(2):
        parts = []
        for t0 in range(0, ctx, 4 * tchunk):
            size = min(4 * tchunk, ctx - t0)
            parts.append(
                load(kv_hbm.at[c, pl.ds(t0, size)], kv_v.at[c, pl.ds(t0, size)])
            )
        kv_load.append(parts)
    wo_load = load(wout_hbm, wo_v)

    pad = chunks * tchunk - ctx
    if pad:
        kv_v[:, ctx:] = jnp.zeros((2, pad) + kv_v.shape[2:], BF16)
    fr_all[mt] = frames_ref[...]
    send_m[...], unsend_m[...], collect_m[...], uncollect_m[...], limit_m[...] = routing(
        me, n, heads, cap, msg, rows, slots, fs_ref.shape[1],
        fs_ref[...], owner_ref[...].astype(F32), length_ref[...].astype(F32),
    )

    for copy in ag:
        copy.wait()
    square = jnp.zeros((rows, 1), F32)
    for b in range(tp):
        wide = fr_all[b].astype(F32)
        square += jnp.sum(wide * wide, axis=1, keepdims=True)
    scale = lax.rsqrt(square * (1.0 / d_all) + 1e-05)
    for b in range(tp):
        gain = gain_ref[:, b * dl : (b + 1) * dl].astype(F32)
        part = (fr_all[b].astype(F32) * scale * gain).astype(BF16)
        for k in range(dl // kc):
            normed[b * (dl // kc) + k] = part[:, k * kc : (k + 1) * kc]

    def project(c):
        w_load[c].wait()

        def step(k, total):
            block = w_v[c, pl.ds(pl.multiple_of(k * kc, kc), kc), :]
            return total + jnp.dot(normed[k], block, preferred_element_type=F32)

        out = lax.fori_loop(
            0, d_all // kc, step, jnp.zeros((rows, heads * HD), F32), unroll=2
        ).astype(BF16)
        stacked = jnp.concatenate([out[:, h * HD : (h + 1) * HD] for h in range(heads)], axis=0)
        placed = jnp.dot(send_m[...], stacked, preferred_element_type=F32)
        return placed.astype(BF16).reshape(n, msg, HD)

    q_send[...] = project(0)
    q_copies = over_sess(q_send, q_recv, q_s, q_r)
    q_recv[me] = q_send[me]
    kv_send[:, 0] = project(1)
    kv_send[:, 1] = project(2)
    kv_copies = over_sess(kv_send, kv_recv, kv_s, kv_r)
    kv_recv[me] = kv_send[me]

    def collected(block):
        return jnp.dot(
            collect_m[...], block.reshape(n * msg, HD), preferred_element_type=F32
        )

    factor = 1.0 / jnp.sqrt(jnp.float32(HD))
    held = heads * slots
    for copy in q_copies:
        copy.wait()
    query = collected(q_recv[...])
    head_row = quot(iota(held, HD, 0), slots)
    query_wide = jnp.concatenate(
        [jnp.where(head_row == h, query, 0.0) for h in range(heads)], axis=1
    ).astype(BF16)
    for copy in kv_load[0]:
        copy.wait()
    width = tchunk * slots
    tiles = width // LANES
    tile_t = LANES // slots
    limit = limit_m[...]

    def score_step(c, top):
        keys = kv_v[0, pl.ds(c * tchunk, tchunk)].reshape(width, heads * HD)
        s = lax.dot_general(
            query_wide, keys, (((1,), (1,)), ((), ())), preferred_element_type=F32
        )
        for k in range(tiles):
            edge = (c * tchunk + k * tile_t).astype(F32)
            tile = jnp.where(
                limit > edge, s[:, k * LANES : (k + 1) * LANES] * factor, -jnp.inf
            )
            scores[c, :, k * LANES : (k + 1) * LANES] = tile
            top = jnp.maximum(top, tile)
        return top

    top = lax.fori_loop(0, chunks, score_step, jnp.full((held, LANES), -jnp.inf, F32))

    for copy in kv_copies:
        copy.wait()
    new_key = collected(kv_recv[:, 0])
    new_value = collected(kv_recv[:, 1])
    own = jnp.sum(query * new_key, axis=1, keepdims=True) * factor
    top = jnp.maximum(jnp.max(top, axis=1, keepdims=True), own)
    top_wide = jnp.broadcast_to(top, (held, LANES))

    def exp_step(c, total):
        for k in range(tiles):
            e = jnp.exp(scores[c, :, k * LANES : (k + 1) * LANES] - top_wide)
            scores[c, :, k * LANES : (k + 1) * LANES] = e
            total = total + e
        return total

    total = lax.fori_loop(0, chunks, exp_step, jnp.zeros((held, LANES), F32))
    own_exp = jnp.exp(own - top)
    total = jnp.sum(total, axis=1, keepdims=True) + own_exp
    inverse = 1.0 / total
    own_weight = (own_exp * inverse).astype(BF16).astype(F32)

    for copy in kv_load[1]:
        copy.wait()
    acc[...] = jnp.zeros_like(acc)

    def mix_step(c, carry):
        weights = (scores[c] * inverse).astype(BF16)
        values = kv_v[1, pl.ds(c * tchunk, tchunk)].reshape(width, heads * HD)
        acc[...] += jnp.dot(weights, values, preferred_element_type=F32)
        return carry

    lax.fori_loop(0, chunks, mix_step, 0)
    mixed = jnp.concatenate(
        [acc[h * slots : (h + 1) * slots, h * HD : (h + 1) * HD] for h in range(heads)], axis=0
    )
    attended = (mixed + own_weight * new_value).astype(BF16)
    r_send[...] = (
        jnp.dot(uncollect_m[...], attended, preferred_element_type=F32)
        .astype(BF16)
        .reshape(n, msg, HD)
    )
    r_copies = over_sess(r_send, r_recv, r_s, r_r)
    r_recv[me] = r_send[me]
    wo_load.wait()
    for copy in r_copies:
        copy.wait()
    back = jnp.dot(
        unsend_m[...], r_recv[...].reshape(n * msg, HD), preferred_element_type=F32
    ).astype(BF16)
    mine = jnp.concatenate([back[h * rows : (h + 1) * rows] for h in range(heads)], axis=1)

    def branch(dest):
        block = wo_v[:, pl.ds(pl.multiple_of(dest * dl, dl), dl)]
        return jnp.dot(mine, block, preferred_element_type=F32)

    p_copies = []
    for d in range(1, tp):
        p_send[d - 1] = branch(tp_peer[d]).astype(BF16)
        p_copies.append(over_tp(p_send.at[d - 1], p_recv.at[d - 1], p_s, p_r, d))
    result = branch(mt)
    for d in range(1, tp):
        p_copies[d - 1].wait()
        result = result + p_recv[d - 1].astype(F32)
    out_ref[...] = (frames_ref[...].astype(F32) + result).astype(BF16)


def body(frames, norm_gain, w_qkv, w_out, kv_cache, frame_session, owner_of, context_len):
    n, tp = lax.axis_size("sess"), lax.axis_size("tp")
    rows, dl = frames.shape
    d_all, head_cols = w_qkv.shape[1:]
    slots, ctx = kv_cache.shape[1:3]
    sessions = frame_session.shape[0]
    heads = head_cols // HD
    cap = (slots + n - 1) // n
    msg = (heads * cap + 15) // 16 * 16
    tchunk = 1024 // slots
    chunks = (ctx + tchunk - 1) // tchunk
    kc = min(512, dl)
    held, total, stack = heads * slots, n * msg, heads * rows
    parts = (ctx + 4 * tchunk - 1) // (4 * tchunk)
    dims = (n, tp, heads, cap, msg, rows, slots, ctx, tchunk, chunks, kc)
    vmem = pl.BlockSpec(memory_space=pltpu.VMEM)
    hbm = pl.BlockSpec(memory_space=pl.ANY)
    dma = pltpu.SemaphoreType.DMA
    return pl.pallas_call(
        functools.partial(kernel, dims),
        out_shape=jax.ShapeDtypeStruct((rows, dl), BF16),
        in_specs=[vmem] * 5 + [hbm] * 3,
        out_specs=vmem,
        scratch_shapes=[
            pltpu.VMEM((3, d_all, head_cols), BF16),
            pltpu.VMEM((head_cols, d_all), BF16),
            pltpu.VMEM((2, chunks * tchunk, slots, head_cols), BF16),
            pltpu.VMEM((tp, rows, dl), BF16),
            pltpu.VMEM((d_all // kc, rows, kc), BF16),
            pltpu.VMEM((n, msg, HD), BF16),
            pltpu.VMEM((n, msg, HD), BF16),
            pltpu.VMEM((n, 2, msg, HD), BF16),
            pltpu.VMEM((n, 2, msg, HD), BF16),
            pltpu.VMEM((n, msg, HD), BF16),
            pltpu.VMEM((n, msg, HD), BF16),
            pltpu.VMEM((tp - 1, rows, dl), BF16),
            pltpu.VMEM((tp - 1, rows, dl), BF16),
            pltpu.VMEM((chunks, held, tchunk * slots), F32),
            pltpu.VMEM((held, head_cols), F32),
            pltpu.VMEM((total, stack), BF16),
            pltpu.VMEM((stack, total), BF16),
            pltpu.VMEM((held, total), BF16),
            pltpu.VMEM((total, held), BF16),
            pltpu.VMEM((held, LANES), F32),
            dma((3 + 2 * parts + 1,)),
            dma((tp - 1,)), dma((tp - 1,)),
            dma((n - 1,)), dma((n - 1,)),
            dma((n - 1,)), dma((n - 1,)),
            dma((n - 1,)), dma((n - 1,)),
            dma((tp - 1,)), dma((tp - 1,)),
        ],
        compiler_params=pltpu.CompilerParams(
            collective_id=0, has_side_effects=True, vmem_limit_bytes=60 * 1024 * 1024
        ),
        name="attention_step",
    )(
        frames,
        norm_gain.reshape(1, d_all),
        frame_session.reshape(1, sessions),
        owner_of.reshape(1, sessions),
        context_len.reshape(1, sessions),
        w_qkv,
        w_out,
        jnp.transpose(kv_cache, (0, 2, 1, 3)),
    )


def solution(mesh):
    in_specs = (
        P("sess", "tp"),
        P(),
        P(None, None, "tp"),
        P("tp", None),
        P(None, "sess", None, "tp"),
        P(),
        P(),
        P(),
    )
    out_specs = P("sess", "tp")
    return jax.shard_map(body, mesh=mesh, in_specs=in_specs, out_specs=out_specs, check_vma=False)
```

profile of v0, /device:TPU:0, one launch (start us, length us, event | category | flops | bytes accessed | tf_op | source)
XLA Modules:
  0.0 37.9 jit_solution(4409291319239617919)
XLA Ops:
  0.0 1.3 %reshape.12.gain_ref = bf16[1,4096]{1,0:T(2,128)(2,1)} reshape(bf16[4096]{0:T(1024)(128)(2,1)} %param.9) | data formatting | bytes 16384 | tf_op jit(solution)/shard_map/reshape | solution.py:366
  1.3 35.2 %attention_step.1 = bf16[16,1024]{1,0:T(8,128)(2,1)} custom-call(bf16[16,1024]{1,0:T(8,128)(2,1)} %frames_ref.1, bf16[1,4096]{1,0:T(2,128)(2,1)} %reshape.12.gain_ref, s32[1,128]{1,0:T(1,128)} %bitcast.5, s32[1,128]{1,0:T(1,128)} %bitcast.6, s32[1,128]{1,0:T(1,128)} %bitcast.7, bf16[3,4096,512]{2,1,0:T(8,128)(2,1)} %wqkv_hbm.1, bf16[512,4096]{1,0:T(8,128)(2,1)} %wout_hbm.1, ...), custom_call_target="tpu_custom_call" | custom-call | tf_op jit(solution)/shard_map/attention_step/pallas_call | solution.py:327
  36.5 1.4 %copy.10 = bf16[16,1024]{1,0:T(8,128)(2,1)} copy(bf16[16,1024]{1,0:T(8,128)(2,1)} %attention_step.1) | data formatting | bytes 65536
where the time goes:
time: 38.2 us; the launch traced here: 37.9 us
  Pallas kernels  35.2 us (92%)
  local copies, waits for them, and re-layouts  2.69 us (7%)
    pallas_call x1, Pallas kernels, body(): pl.pallas_call(functools.partial(kernel, dims), out_shape=jax.ShapeDtypeS...  35.2 us
    unnamed x1, local copies, waits for them, and re-layouts  1.38 us
    reshape x1, local copies, waits for them, and re-layouts, body(): norm_gain.reshape(1, d_all)  1.31 us

commit v1 on v0

--- a/solution.py
+++ b/solution.py
@@ -98,14 +98,14 @@
 
 def kernel(
     dims,
-    frames_ref, gain_ref, fs_ref, owner_ref, length_ref, wqkv_hbm, wout_hbm, kv_hbm,
+    frames_hbm, gain_hbm, fs_hbm, owner_hbm, length_hbm, wqkv_hbm, wout_hbm, kv_hbm,
     out_ref,
-    w_v, wo_v, kv_v, fr_all, normed, q_send, q_recv, kv_send, kv_recv, r_send, r_recv,
+    gain_v, fs_v, owner_v, length_v, w_v, wo_v, kv_v, fr_all, normed, q_send, q_recv, kv_send, kv_recv, r_send, r_recv,
     p_send, p_recv, scores, acc, send_m, unsend_m, collect_m, uncollect_m, limit_m,
     load_sem, ag_s, ag_r, q_s, q_r, kv_s, kv_r, r_s, r_r, p_s, p_r,
 ):
     n, tp, heads, cap, msg, rows, slots, ctx, tchunk, chunks, kc = dims
-    dl = frames_ref.shape[1]
+    dl = frames_hbm.shape[1]
     d_all = dl * tp
     me, mt = lax.axis_index("sess"), lax.axis_index("tp")
     sess_peer = [lax.rem(me + d, n) for d in range(n)]
@@ -117,14 +117,20 @@
         loads.append(pltpu.make_async_copy(src, dst, load_sem.at[len(loads)]))
         loads[-1].start()
         return loads[-1]
-
-    w_load = [load(wqkv_hbm.at[c], w_v.at[c]) for c in range(3)]
 
     barrier = pltpu.get_barrier_semaphore()
     for d in range(1, tp):
         pl.semaphore_signal(barrier, inc=1, device_id=(me, tp_peer[d]), device_id_type=MESH)
     for d in range(1, n):
         pl.semaphore_signal(barrier, inc=1, device_id=(sess_peer[d], mt), device_id_type=MESH)
+    small = [
+        load(fs_hbm, fs_v),
+        load(owner_hbm, owner_v),
+        load(length_hbm, length_v),
+        load(gain_hbm, gain_v),
+        load(frames_hbm, fr_all.at[mt]),
+    ]
+    w_load = [load(wqkv_hbm.at[c], w_v.at[c]) for c in range(3)]
     pl.semaphore_wait(barrier, n + tp - 2)
 
     def over_tp(src, dst, s, r, d):
@@ -147,7 +153,7 @@
             copies.append(copy)
         return copies
 
-    ag = [over_tp(frames_ref, fr_all.at[mt], ag_s, ag_r, d) for d in range(1, tp)]
+    ag = [over_tp(frames_hbm, fr_all.at[mt], ag_s, ag_r, d) for d in range(1, tp)]
     kv_load = []
     for c in range(2):
         parts = []
@@ -162,10 +168,11 @@
     pad = chunks * tchunk - ctx
     if pad:
         kv_v[:, ctx:] = jnp.zeros((2, pad) + kv_v.shape[2:], BF16)
-    fr_all[mt] = frames_ref[...]
+    for copy in small:
+        copy.wait()
     send_m[...], unsend_m[...], collect_m[...], uncollect_m[...], limit_m[...] = routing(
-        me, n, heads, cap, msg, rows, slots, fs_ref.shape[1],
-        fs_ref[...], owner_ref[...].astype(F32), length_ref[...].astype(F32),
+        me, n, heads, cap, msg, rows, slots, fs_v.shape[1],
+        fs_v[...], owner_v[...].astype(F32), length_v[...].astype(F32),
     )
 
     for copy in ag:
@@ -175,11 +182,13 @@
         wide = fr_all[b].astype(F32)
         square += jnp.sum(wide * wide, axis=1, keepdims=True)
     scale = lax.rsqrt(square * (1.0 / d_all) + 1e-05)
+    gain = gain_v[...].astype(F32)
     for b in range(tp):
-        gain = gain_ref[:, b * dl : (b + 1) * dl].astype(F32)
-        part = (fr_all[b].astype(F32) * scale * gain).astype(BF16)
-        for k in range(dl // kc):
-            normed[b * (dl // kc) + k] = part[:, k * kc : (k + 1) * kc]
+        for t in range(dl // LANES):
+            col = b * dl + t * LANES
+            part = fr_all[b, :, t * LANES : (t + 1) * LANES].astype(F32) * scale
+            part = part * gain[col // LANES : col // LANES + 1]
+            normed[col // kc, :, col % kc : col % kc + LANES] = part.astype(BF16)
 
     def project(c):
         w_load[c].wait()
@@ -189,7 +198,7 @@
             return total + jnp.dot(normed[k], block, preferred_element_type=F32)
 
         out = lax.fori_loop(
-            0, d_all // kc, step, jnp.zeros((rows, heads * HD), F32), unroll=2
+            0, d_all // kc, step, jnp.zeros((rows, heads * HD), F32), unroll=4
         ).astype(BF16)
         stacked = jnp.concatenate([out[:, h * HD : (h + 1) * HD] for h in range(heads)], axis=0)
         placed = jnp.dot(send_m[...], stacked, preferred_element_type=F32)
@@ -238,7 +247,7 @@
             top = jnp.maximum(top, tile)
         return top
 
-    top = lax.fori_loop(0, chunks, score_step, jnp.full((held, LANES), -jnp.inf, F32))
+    top = lax.fori_loop(0, chunks, score_step, jnp.full((held, LANES), -jnp.inf, F32), unroll=2)
 
     for copy in kv_copies:
         copy.wait()
@@ -248,34 +257,30 @@
     top = jnp.maximum(jnp.max(top, axis=1, keepdims=True), own)
     top_wide = jnp.broadcast_to(top, (held, LANES))
 
-    def exp_step(c, total):
+    for copy in kv_load[1]:
+        copy.wait()
+    acc[...] = jnp.zeros_like(acc)
+
+    def mix_step(c, total):
+        weights = []
         for k in range(tiles):
             e = jnp.exp(scores[c, :, k * LANES : (k + 1) * LANES] - top_wide)
-            scores[c, :, k * LANES : (k + 1) * LANES] = e
             total = total + e
+            weights.append(e.astype(BF16))
+        values = kv_v[1, pl.ds(c * tchunk, tchunk)].reshape(width, heads * HD)
+        acc[...] += jnp.dot(
+            jnp.concatenate(weights, axis=1), values, preferred_element_type=F32
+        )
         return total
 
-    total = lax.fori_loop(0, chunks, exp_step, jnp.zeros((held, LANES), F32))
+    total = lax.fori_loop(0, chunks, mix_step, jnp.zeros((held, LANES), F32), unroll=2)
     own_exp = jnp.exp(own - top)
-    total = jnp.sum(total, axis=1, keepdims=True) + own_exp
-    inverse = 1.0 / total
-    own_weight = (own_exp * inverse).astype(BF16).astype(F32)
-
-    for copy in kv_load[1]:
-        copy.wait()
-    acc[...] = jnp.zeros_like(acc)
-
-    def mix_step(c, carry):
-        weights = (scores[c] * inverse).astype(BF16)
-        values = kv_v[1, pl.ds(c * tchunk, tchunk)].reshape(width, heads * HD)
-        acc[...] += jnp.dot(weights, values, preferred_element_type=F32)
-        return carry
-
-    lax.fori_loop(0, chunks, mix_step, 0)
+    inverse = 1.0 / (jnp.sum(total, axis=1, keepdims=True) + own_exp)
+    own_weight = own_exp.astype(BF16).astype(F32)
     mixed = jnp.concatenate(
         [acc[h * slots : (h + 1) * slots, h * HD : (h + 1) * HD] for h in range(heads)], axis=0
     )
-    attended = (mixed + own_weight * new_value).astype(BF16)
+    attended = ((mixed + own_weight * new_value) * inverse).astype(BF16)
     r_send[...] = (
         jnp.dot(uncollect_m[...], attended, preferred_element_type=F32)
         .astype(BF16)
@@ -303,7 +308,7 @@
     for d in range(1, tp):
         p_copies[d - 1].wait()
         result = result + p_recv[d - 1].astype(F32)
-    out_ref[...] = (frames_ref[...].astype(F32) + result).astype(BF16)
+    out_ref[...] = (fr_all[mt].astype(F32) + result).astype(BF16)
 
 
 def body(frames, norm_gain, w_qkv, w_out, kv_cache, frame_session, owner_of, context_len):
@@ -326,10 +331,14 @@
     dma = pltpu.SemaphoreType.DMA
     return pl.pallas_call(
         functools.partial(kernel, dims),
-        out_shape=jax.ShapeDtypeStruct((rows, dl), BF16),
-        in_specs=[vmem] * 5 + [hbm] * 3,
+        out_shape=pltpu.VMEM((rows, dl), BF16),
+        in_specs=[hbm] * 8,
         out_specs=vmem,
         scratch_shapes=[
+            pltpu.VMEM((d_all // LANES, LANES), BF16),
+            pltpu.VMEM((1, sessions), jnp.int32),
+            pltpu.VMEM((1, sessions), jnp.int32),
+            pltpu.VMEM((1, sessions), jnp.int32),
             pltpu.VMEM((3, d_all, head_cols), BF16),
             pltpu.VMEM((head_cols, d_all), BF16),
             pltpu.VMEM((2, chunks * tchunk, slots, head_cols), BF16),
@@ -350,7 +359,7 @@
             pltpu.VMEM((held, total), BF16),
             pltpu.VMEM((total, held), BF16),
             pltpu.VMEM((held, LANES), F32),
-            dma((3 + 2 * parts + 1,)),
+            dma((5 + 3 + 2 * parts + 1,)),
             dma((tp - 1,)), dma((tp - 1,)),
             dma((n - 1,)), dma((n - 1,)),
             dma((n - 1,)), dma((n - 1,)),
@@ -363,7 +372,7 @@
         name="attention_step",
     )(
         frames,
-        norm_gain.reshape(1, d_all),
+        norm_gain.reshape(d_all // LANES, LANES),
         frame_session.reshape(1, sessions),
         owner_of.reshape(1, sessions),
         context_len.reshape(1, sessions),

time: 38.2 us -> 31.4 us (0.82)
  Pallas kernels: 35.2 us -> 30.7 us
  local copies, waits for them, and re-layouts: 2.69 us -> 0.62 us
    pallas_call x1, Pallas kernels: 35.2 us -> 30.7 us  [body(): pl.pallas_call(functools.partial(kernel, dims), out_shape=pltpu.VMEM((row...]
    reshape x1 -> x0, local copies, waits for them, and re-layouts: 1.31 us -> none  [body(): norm_gain.reshape(1, d_all)]
    unnamed x1, local copies, waits for them, and re-layouts: 1.38 us -> 0.62 us
where the time goes in v1:
time: 31.4 us; the launch traced here: 31.3 us
  Pallas kernels  30.7 us (98%)
  local copies, waits for them, and re-layouts  0.62 us (2%)
    pallas_call x1, Pallas kernels, body(): pl.pallas_call(functools.partial(kernel, dims), out_shape=pltpu.VMEM((row...  30.7 us

profile of v1, /device:TPU:0, one launch (start us, length us, event | category | flops | bytes accessed | tf_op | source)
XLA Modules:
  0.0 31.3 jit_solution(16652414249332782416)
XLA Ops:
  0.0 30.7 %attention_step.1 = bf16[16,1024]{1,0:T(8,128)(2,1)S(1)} custom-call(bf16[16,1024]{1,0:T(8,128)(2,1)} %frames_hbm.1, bf16[32,128]{1,0:T(8,128)(2,1)} %bitcast.6, s32[1,128]{1,0:T(1,128)} %bitcast.7, s32[1,128]{1,0:T(1,128)} %bitcast.8, s32[1,128]{1,0:T(1,128)} %bitcast.9, bf16[3,4096,512]{2,1,0:T(8,128)(2,1)} %wqkv_hbm.1, bf16[512,4096]{1,0:T(8,128)(2,1)} %wout_hbm.1, ...), custom_call_target="tpu_custom_call" | custom-call | tf_op jit(solution)/shard_map/attention_step/pallas_call | solution.py:332
  30.7 0.6 %copy.10 = bf16[16,1024]{1,0:T(8,128)(2,1)} copy(bf16[16,1024]{1,0:T(8,128)(2,1)S(1)} %attention_step.1) | data formatting | bytes 65536

commit v2 on v1

--- a/solution.py
+++ b/solution.py
@@ -130,7 +130,7 @@
         load(gain_hbm, gain_v),
         load(frames_hbm, fr_all.at[mt]),
     ]
-    w_load = [load(wqkv_hbm.at[c], w_v.at[c]) for c in range(3)]
+    w_load = [load(wqkv_hbm.at[0], w_v.at[0])]
     pl.semaphore_wait(barrier, n + tp - 2)
 
     def over_tp(src, dst, s, r, d):
@@ -154,17 +154,22 @@
         return copies
 
     ag = [over_tp(frames_hbm, fr_all.at[mt], ag_s, ag_r, d) for d in range(1, tp)]
-    kv_load = []
-    for c in range(2):
+    w_load += [load(wqkv_hbm.at[c], w_v.at[c]) for c in (1, 2)]
+
+    def load_cache(c):
         parts = []
         for t0 in range(0, ctx, 4 * tchunk):
-            size = min(4 * tchunk, ctx - t0)
-            parts.append(
-                load(kv_hbm.at[c, pl.ds(t0, size)], kv_v.at[c, pl.ds(t0, size)])
-            )
-        kv_load.append(parts)
-    wo_load = load(wout_hbm, wo_v)
-
+            span = pl.ds(t0, min(4 * tchunk, ctx - t0))
+            parts.append(load(kv_hbm.at[c, span], kv_v.at[c, span]))
+        return parts
+
+    def over_cache(parts, step, carry):
+        for i, copy in enumerate(parts):
+            copy.wait()
+            carry = lax.fori_loop(4 * i, min(4 * i + 4, chunks), step, carry, unroll=2)
+        return carry
+
+    key_load = load_cache(0)
     pad = chunks * tchunk - ctx
     if pad:
         kv_v[:, ctx:] = jnp.zeros((2, pad) + kv_v.shape[2:], BF16)
@@ -206,10 +211,12 @@
 
     q_send[...] = project(0)
     q_copies = over_sess(q_send, q_recv, q_s, q_r)
+    value_load = load_cache(1)
     q_recv[me] = q_send[me]
     kv_send[:, 0] = project(1)
     kv_send[:, 1] = project(2)
     kv_copies = over_sess(kv_send, kv_recv, kv_s, kv_r)
+    wo_load = load(wout_hbm, wo_v)
     kv_recv[me] = kv_send[me]
 
     def collected(block):
@@ -226,8 +233,6 @@
     query_wide = jnp.concatenate(
         [jnp.where(head_row == h, query, 0.0) for h in range(heads)], axis=1
     ).astype(BF16)
-    for copy in kv_load[0]:
-        copy.wait()
     width = tchunk * slots
     tiles = width // LANES
     tile_t = LANES // slots
@@ -247,7 +252,7 @@
             top = jnp.maximum(top, tile)
         return top
 
-    top = lax.fori_loop(0, chunks, score_step, jnp.full((held, LANES), -jnp.inf, F32), unroll=2)
+    top = over_cache(key_load, score_step, jnp.full((held, LANES), -jnp.inf, F32))
 
     for copy in kv_copies:
         copy.wait()
@@ -257,8 +262,6 @@
     top = jnp.maximum(jnp.max(top, axis=1, keepdims=True), own)
     top_wide = jnp.broadcast_to(top, (held, LANES))
 
-    for copy in kv_load[1]:
-        copy.wait()
     acc[...] = jnp.zeros_like(acc)
 
     def mix_step(c, total):
@@ -273,7 +276,7 @@
         )
         return total
 
-    total = lax.fori_loop(0, chunks, mix_step, jnp.zeros((held, LANES), F32), unroll=2)
+    total = over_cache(value_load, mix_step, jnp.zeros((held, LANES), F32))
     own_exp = jnp.exp(own - top)
     inverse = 1.0 / (jnp.sum(total, axis=1, keepdims=True) + own_exp)
     own_weight = own_exp.astype(BF16).astype(F32)

time: 31.4 us -> 31.4 us (level)
  no operation moved by 1% of the time
where the time goes in v2:
time: 31.4 us; the launch traced here: 31.3 us
  Pallas kernels  30.7 us (98%)
  local copies, waits for them, and re-layouts  0.62 us (2%)
    pallas_call x1, Pallas kernels, body(): pl.pallas_call(functools.partial(kernel, dims), out_shape=pltpu.VMEM((row...  30.7 us

profile of v2, /device:TPU:0, one launch (start us, length us, event | category | flops | bytes accessed | tf_op | source)
XLA Modules:
  0.0 31.3 jit_solution(6338299543431557191)
XLA Ops:
  0.0 30.7 %attention_step.1 = bf16[16,1024]{1,0:T(8,128)(2,1)S(1)} custom-call(bf16[16,1024]{1,0:T(8,128)(2,1)} %frames_hbm.1, bf16[32,128]{1,0:T(8,128)(2,1)} %bitcast.6, s32[1,128]{1,0:T(1,128)} %bitcast.7, s32[1,128]{1,0:T(1,128)} %bitcast.8, s32[1,128]{1,0:T(1,128)} %bitcast.9, bf16[3,4096,512]{2,1,0:T(8,128)(2,1)} %wqkv_hbm.1, bf16[512,4096]{1,0:T(8,128)(2,1)} %wout_hbm.1, ...), custom_call_target="tpu_custom_call" | custom-call | tf_op jit(solution)/shard_map/attention_step/pallas_call | solution.py:335
  30.7 0.6 %copy.10 = bf16[16,1024]{1,0:T(8,128)(2,1)} copy(bf16[16,1024]{1,0:T(8,128)(2,1)S(1)} %attention_step.1) | data formatting | bytes 65536

commit v3 on v2

--- a/solution.py
+++ b/solution.py
@@ -104,7 +104,7 @@
     p_send, p_recv, scores, acc, send_m, unsend_m, collect_m, uncollect_m, limit_m,
     load_sem, ag_s, ag_r, q_s, q_r, kv_s, kv_r, r_s, r_r, p_s, p_r,
 ):
-    n, tp, heads, cap, msg, rows, slots, ctx, tchunk, chunks, kc = dims
+    n, tp, heads, cap, msg, rows, slots, ctx, tchunk, chunks = dims
     dl = frames_hbm.shape[1]
     d_all = dl * tp
     me, mt = lax.axis_index("sess"), lax.axis_index("tp")
@@ -163,12 +163,6 @@
             parts.append(load(kv_hbm.at[c, span], kv_v.at[c, span]))
         return parts
 
-    def over_cache(parts, step, carry):
-        for i, copy in enumerate(parts):
-            copy.wait()
-            carry = lax.fori_loop(4 * i, min(4 * i + 4, chunks), step, carry, unroll=2)
-        return carry
-
     key_load = load_cache(0)
     pad = chunks * tchunk - ctx
     if pad:
@@ -193,18 +187,12 @@
             col = b * dl + t * LANES
             part = fr_all[b, :, t * LANES : (t + 1) * LANES].astype(F32) * scale
             part = part * gain[col // LANES : col // LANES + 1]
-            normed[col // kc, :, col % kc : col % kc + LANES] = part.astype(BF16)
+            normed[:, col : col + LANES] = part.astype(BF16)
 
     def project(c):
         w_load[c].wait()
 
-        def step(k, total):
-            block = w_v[c, pl.ds(pl.multiple_of(k * kc, kc), kc), :]
-            return total + jnp.dot(normed[k], block, preferred_element_type=F32)
-
-        out = lax.fori_loop(
-            0, d_all // kc, step, jnp.zeros((rows, heads * HD), F32), unroll=4
-        ).astype(BF16)
+        out = jnp.dot(normed[...], w_v[c], preferred_element_type=F32).astype(BF16)
         stacked = jnp.concatenate([out[:, h * HD : (h + 1) * HD] for h in range(heads)], axis=0)
         placed = jnp.dot(send_m[...], stacked, preferred_element_type=F32)
         return placed.astype(BF16).reshape(n, msg, HD)
@@ -244,7 +232,7 @@
             query_wide, keys, (((1,), (1,)), ((), ())), preferred_element_type=F32
         )
         for k in range(tiles):
-            edge = (c * tchunk + k * tile_t).astype(F32)
+            edge = float(c * tchunk + k * tile_t)
             tile = jnp.where(
                 limit > edge, s[:, k * LANES : (k + 1) * LANES] * factor, -jnp.inf
             )
@@ -252,7 +240,11 @@
             top = jnp.maximum(top, tile)
         return top
 
-    top = over_cache(key_load, score_step, jnp.full((held, LANES), -jnp.inf, F32))
+    top = jnp.full((held, LANES), -jnp.inf, F32)
+    for i, copy in enumerate(key_load):
+        copy.wait()
+        for c in range(4 * i, min(4 * i + 4, chunks)):
+            top = score_step(c, top)
 
     for copy in kv_copies:
         copy.wait()
@@ -262,21 +254,19 @@
     top = jnp.maximum(jnp.max(top, axis=1, keepdims=True), own)
     top_wide = jnp.broadcast_to(top, (held, LANES))
 
-    acc[...] = jnp.zeros_like(acc)
-
-    def mix_step(c, total):
+    total = jnp.zeros((held, LANES), F32)
+    for i, copy in enumerate(value_load):
         weights = []
-        for k in range(tiles):
-            e = jnp.exp(scores[c, :, k * LANES : (k + 1) * LANES] - top_wide)
-            total = total + e
-            weights.append(e.astype(BF16))
-        values = kv_v[1, pl.ds(c * tchunk, tchunk)].reshape(width, heads * HD)
-        acc[...] += jnp.dot(
-            jnp.concatenate(weights, axis=1), values, preferred_element_type=F32
-        )
-        return total
-
-    total = over_cache(value_load, mix_step, jnp.zeros((held, LANES), F32))
+        for c in range(4 * i, min(4 * i + 4, chunks)):
+            for k in range(tiles):
+                e = jnp.exp(scores[c, :, k * LANES : (k + 1) * LANES] - top_wide)
+                total = total + e
+                weights.append(e.astype(BF16))
+        copy.wait()
+        span = len(weights) * LANES
+        values = kv_v[1, pl.ds(4 * i * tchunk, span // slots)].reshape(span, heads * HD)
+        part = jnp.dot(jnp.concatenate(weights, axis=1), values, preferred_element_type=F32)
+        acc[...] = part if i == 0 else acc[...] + part
     own_exp = jnp.exp(own - top)
     inverse = 1.0 / (jnp.sum(total, axis=1, keepdims=True) + own_exp)
     own_weight = own_exp.astype(BF16).astype(F32)
@@ -325,10 +315,9 @@
     msg = (heads * cap + 15) // 16 * 16
     tchunk = 1024 // slots
     chunks = (ctx + tchunk - 1) // tchunk
-    kc = min(512, dl)
     held, total, stack = heads * slots, n * msg, heads * rows
     parts = (ctx + 4 * tchunk - 1) // (4 * tchunk)
-    dims = (n, tp, heads, cap, msg, rows, slots, ctx, tchunk, chunks, kc)
+    dims = (n, tp, heads, cap, msg, rows, slots, ctx, tchunk, chunks)
     vmem = pl.BlockSpec(memory_space=pltpu.VMEM)
     hbm = pl.BlockSpec(memory_space=pl.ANY)
     dma = pltpu.SemaphoreType.DMA
@@ -346,7 +335,7 @@
             pltpu.VMEM((head_cols, d_all), BF16),
             pltpu.VMEM((2, chunks * tchunk, slots, head_cols), BF16),
             pltpu.VMEM((tp, rows, dl), BF16),
-            pltpu.VMEM((d_all // kc, rows, kc), BF16),
+            pltpu.VMEM((rows, d_all), BF16),
             pltpu.VMEM((n, msg, HD), BF16),
             pltpu.VMEM((n, msg, HD), BF16),
             pltpu.VMEM((n, 2, msg, HD), BF16),

time: 31.4 us -> 31 us (0.987)
  Pallas kernels: 30.7 us -> 30.2 us
    pallas_call x1, Pallas kernels: 30.7 us -> 30.2 us  [body(): pl.pallas_call(functools.partial(kernel, dims), out_shape=pltpu.VMEM((row...]
where the time goes in v3:
time: 31 us; the launch traced here: 30.8 us
  Pallas kernels  30.2 us (97%)
  local copies, waits for them, and re-layouts  0.62 us (2%)
    pallas_call x1, Pallas kernels, body(): pl.pallas_call(functools.partial(kernel, dims), out_shape=pltpu.VMEM((row...  30.2 us

profile of v3, /device:TPU:0, one launch (start us, length us, event | category | flops | bytes accessed | tf_op | source)
XLA Modules:
  0.0 30.8 jit_solution(12041416883268597522)
XLA Ops:
  0.0 30.2 %attention_step.1 = bf16[16,1024]{1,0:T(8,128)(2,1)S(1)} custom-call(bf16[16,1024]{1,0:T(8,128)(2,1)} %frames_hbm.1, bf16[32,128]{1,0:T(8,128)(2,1)} %bitcast.6, s32[1,128]{1,0:T(1,128)} %bitcast.7, s32[1,128]{1,0:T(1,128)} %bitcast.8, s32[1,128]{1,0:T(1,128)} %bitcast.9, bf16[3,4096,512]{2,1,0:T(8,128)(2,1)} %wqkv_hbm.1, bf16[512,4096]{1,0:T(8,128)(2,1)} %wout_hbm.1, ...), custom_call_target="tpu_custom_call" | custom-call | tf_op jit(solution)/shard_map/attention_step/pallas_call | solution.py:324
  30.2 0.6 %copy.10 = bf16[16,1024]{1,0:T(8,128)(2,1)} copy(bf16[16,1024]{1,0:T(8,128)(2,1)S(1)} %attention_step.1) | data formatting | bytes 65536

commit v4 on v3

--- a/solution.py
+++ b/solution.py
@@ -217,9 +217,10 @@
     for copy in q_copies:
         copy.wait()
     query = collected(q_recv[...])
-    head_row = quot(iota(held, HD, 0), slots)
+    query_t = query.T
+    head_lane = quot(iota(HD, held, 1), slots)
     query_wide = jnp.concatenate(
-        [jnp.where(head_row == h, query, 0.0) for h in range(heads)], axis=1
+        [jnp.where(head_lane == h, query_t, 0.0) for h in range(heads)], axis=0
     ).astype(BF16)
     width = tchunk * slots
     tiles = width // LANES
@@ -228,13 +229,11 @@
 
     def score_step(c, top):
         keys = kv_v[0, pl.ds(c * tchunk, tchunk)].reshape(width, heads * HD)
-        s = lax.dot_general(
-            query_wide, keys, (((1,), (1,)), ((), ())), preferred_element_type=F32
-        )
+        s = jnp.dot(keys, query_wide, preferred_element_type=F32)
         for k in range(tiles):
             edge = float(c * tchunk + k * tile_t)
             tile = jnp.where(
-                limit > edge, s[:, k * LANES : (k + 1) * LANES] * factor, -jnp.inf
+                limit > edge, s[k * LANES : (k + 1) * LANES].T * factor, -jnp.inf
             )
             scores[c, :, k * LANES : (k + 1) * LANES] = tile
             top = jnp.maximum(top, tile)

time: 31 us -> 30.7 us (level)
  no operation moved by 1% of the time
where the time goes in v4:
time: 30.7 us; the launch traced here: 30.5 us
  Pallas kernels  29.9 us (97%)
  local copies, waits for them, and re-layouts  0.62 us (2%)
    pallas_call x1, Pallas kernels, body(): pl.pallas_call(functools.partial(kernel, dims), out_shape=pltpu.VMEM((row...  29.9 us
    unnamed x1, local copies, waits for them, and re-layouts  0.62 us

profile of v4, /device:TPU:0, one launch (start us, length us, event | category | flops | bytes accessed | tf_op | source)
XLA Modules:
  0.0 30.5 jit_solution(12505888260709737794)
XLA Ops:
  0.0 29.9 %attention_step.1 = bf16[16,1024]{1,0:T(8,128)(2,1)S(1)} custom-call(bf16[16,1024]{1,0:T(8,128)(2,1)} %frames_hbm.1, bf16[32,128]{1,0:T(8,128)(2,1)} %bitcast.6, s32[1,128]{1,0:T(1,128)} %bitcast.7, s32[1,128]{1,0:T(1,128)} %bitcast.8, s32[1,128]{1,0:T(1,128)} %bitcast.9, bf16[3,4096,512]{2,1,0:T(8,128)(2,1)} %wqkv_hbm.1, bf16[512,4096]{1,0:T(8,128)(2,1)} %wout_hbm.1, ...), custom_call_target="tpu_custom_call" | custom-call | tf_op jit(solution)/shard_map/attention_step/pallas_call | solution.py:323
  29.9 0.6 %copy.10 = bf16[16,1024]{1,0:T(8,128)(2,1)} copy(bf16[16,1024]{1,0:T(8,128)(2,1)S(1)} %attention_step.1) | data formatting | bytes 65536

commit v5 on v4

--- a/solution.py
+++ b/solution.py
@@ -67,12 +67,6 @@
     )
     head_i, code = message_code(iota(total, stack, 0))
     send = one_hot((head_i == quot(iota(total, stack, 1), rows)) & (code == local))
-    local_c = pick(
-        iota(stack, sessions, 1) == me * rows + rest(iota(stack, sessions, 0), rows), target, 1
-    )
-    head_i, code = message_code(iota(stack, total, 1))
-    unsend = one_hot((head_i == quot(iota(stack, total, 0), rows)) & (code == local_c))
-
     in_slot = (row_slot == rest(iota(held, sessions, 0), slots).astype(F32)) & (row_owner == me_f)
     _, code = message_code(iota(sessions, total, 1))
     spread = jnp.dot(one_hot(in_slot), one_hot(place_c == code), preferred_element_type=F32)
@@ -93,7 +87,7 @@
         held_len - quot(lane, slots).astype(F32),
         -1.0,
     )
-    return send, unsend, collect, uncollect, limit
+    return send, local, collect, uncollect, limit
 
 
 def kernel(
@@ -101,7 +95,7 @@
     frames_hbm, gain_hbm, fs_hbm, owner_hbm, length_hbm, wqkv_hbm, wout_hbm, kv_hbm,
     out_ref,
     gain_v, fs_v, owner_v, length_v, w_v, wo_v, kv_v, fr_all, normed, q_send, q_recv, kv_send, kv_recv, r_send, r_recv,
-    p_send, p_recv, scores, acc, send_m, unsend_m, collect_m, uncollect_m, limit_m,
+    p_send, p_recv, scores, acc, send_m, collect_m, uncollect_m, limit_m,
     load_sem, ag_s, ag_r, q_s, q_r, kv_s, kv_r, r_s, r_r, p_s, p_r,
 ):
     n, tp, heads, cap, msg, rows, slots, ctx, tchunk, chunks = dims
@@ -131,6 +125,18 @@
         load(frames_hbm, fr_all.at[mt]),
     ]
     w_load = [load(wqkv_hbm.at[0], w_v.at[0])]
+    w_load += [load(wqkv_hbm.at[c], w_v.at[c]) for c in (1, 2)]
+
+    def load_cache(c):
+        parts = []
+        for t0 in range(0, ctx, 2 * tchunk):
+            span = pl.ds(t0, min(2 * tchunk, ctx - t0))
+            parts.append(load(kv_hbm.at[c, span], kv_v.at[c, span]))
+        return parts
+
+    key_load = load_cache(0)
+    value_load = load_cache(1)
+    wo_load = load(wout_hbm, wo_v)
     pl.semaphore_wait(barrier, n + tp - 2)
 
     def over_tp(src, dst, s, r, d):
@@ -154,22 +160,12 @@
         return copies
 
     ag = [over_tp(frames_hbm, fr_all.at[mt], ag_s, ag_r, d) for d in range(1, tp)]
-    w_load += [load(wqkv_hbm.at[c], w_v.at[c]) for c in (1, 2)]
-
-    def load_cache(c):
-        parts = []
-        for t0 in range(0, ctx, 4 * tchunk):
-            span = pl.ds(t0, min(4 * tchunk, ctx - t0))
-            parts.append(load(kv_hbm.at[c, span], kv_v.at[c, span]))
-        return parts
-
-    key_load = load_cache(0)
     pad = chunks * tchunk - ctx
     if pad:
         kv_v[:, ctx:] = jnp.zeros((2, pad) + kv_v.shape[2:], BF16)
     for copy in small:
         copy.wait()
-    send_m[...], unsend_m[...], collect_m[...], uncollect_m[...], limit_m[...] = routing(
+    send_m[...], local, collect_m[...], uncollect_m[...], limit_m[...] = routing(
         me, n, heads, cap, msg, rows, slots, fs_v.shape[1],
         fs_v[...], owner_v[...].astype(F32), length_v[...].astype(F32),
     )
@@ -199,12 +195,10 @@
 
     q_send[...] = project(0)
     q_copies = over_sess(q_send, q_recv, q_s, q_r)
-    value_load = load_cache(1)
     q_recv[me] = q_send[me]
     kv_send[:, 0] = project(1)
     kv_send[:, 1] = project(2)
     kv_copies = over_sess(kv_send, kv_recv, kv_s, kv_r)
-    wo_load = load(wout_hbm, wo_v)
     kv_recv[me] = kv_send[me]
 
     def collected(block):
@@ -242,7 +236,7 @@
     top = jnp.full((held, LANES), -jnp.inf, F32)
     for i, copy in enumerate(key_load):
         copy.wait()
-        for c in range(4 * i, min(4 * i + 4, chunks)):
+        for c in range(2 * i, min(2 * i + 2, chunks)):
             top = score_step(c, top)
 
     for copy in kv_copies:
@@ -256,14 +250,14 @@
     total = jnp.zeros((held, LANES), F32)
     for i, copy in enumerate(value_load):
         weights = []
-        for c in range(4 * i, min(4 * i + 4, chunks)):
+        for c in range(2 * i, min(2 * i + 2, chunks)):
             for k in range(tiles):
                 e = jnp.exp(scores[c, :, k * LANES : (k + 1) * LANES] - top_wide)
                 total = total + e
                 weights.append(e.astype(BF16))
         copy.wait()
         span = len(weights) * LANES
-        values = kv_v[1, pl.ds(4 * i * tchunk, span // slots)].reshape(span, heads * HD)
+        values = kv_v[1, pl.ds(2 * i * tchunk, span // slots)].reshape(span, heads * HD)
         part = jnp.dot(jnp.concatenate(weights, axis=1), values, preferred_element_type=F32)
         acc[...] = part if i == 0 else acc[...] + part
     own_exp = jnp.exp(own - top)
@@ -280,11 +274,19 @@
     )
     r_copies = over_sess(r_send, r_recv, r_s, r_r)
     r_recv[me] = r_send[me]
+    stack, count = heads * rows, n * msg
+    eye = iota(stack, stack, 0) == iota(stack, stack, 1)
+    local_c = jnp.sum(jnp.where(eye, local, 0.0), axis=1, keepdims=True)
+    at = iota(stack, count, 1)
+    inner = rest(at, msg)
+    code = (quot(at, msg) * cap + rest(inner, cap)).astype(F32)
+    same_head = quot(inner, cap) == quot(iota(stack, count, 0), rows)
+    unsend = one_hot(same_head & (code == local_c))
     wo_load.wait()
     for copy in r_copies:
         copy.wait()
     back = jnp.dot(
-        unsend_m[...], r_recv[...].reshape(n * msg, HD), preferred_element_type=F32
+        unsend, r_recv[...].reshape(n * msg, HD), preferred_element_type=F32
     ).astype(BF16)
     mine = jnp.concatenate([back[h * rows : (h + 1) * rows] for h in range(heads)], axis=1)
 
@@ -315,7 +317,7 @@
     tchunk = 1024 // slots
     chunks = (ctx + tchunk - 1) // tchunk
     held, total, stack = heads * slots, n * msg, heads * rows
-    parts = (ctx + 4 * tchunk - 1) // (4 * tchunk)
+    parts = (ctx + 2 * tchunk - 1) // (2 * tchunk)
     dims = (n, tp, heads, cap, msg, rows, slots, ctx, tchunk, chunks)
     vmem = pl.BlockSpec(memory_space=pltpu.VMEM)
     hbm = pl.BlockSpec(memory_space=pl.ANY)
@@ -346,7 +348,6 @@
             pltpu.VMEM((chunks, held, tchunk * slots), F32),
             pltpu.VMEM((held, head_cols), F32),
             pltpu.VMEM((total, stack), BF16),
-            pltpu.VMEM((stack, total), BF16),
             pltpu.VMEM((held, total), BF16),
             pltpu.VMEM((total, held), BF16),
             pltpu.VMEM((held, LANES), F32),

time: 30.7 us -> 31.9 us (1.039)
  Pallas kernels: 29.9 us -> 31.1 us
    pallas_call x1, Pallas kernels: 29.9 us -> 31.1 us  [body(): pl.pallas_call(functools.partial(kernel, dims), out_shape=pltpu.VMEM((row...]
where the time goes in v5:
time: 31.9 us; the launch traced here: 31.7 us
  Pallas kernels  31.1 us (97%)
  local copies, waits for them, and re-layouts  0.62 us (2%)
    pallas_call x1, Pallas kernels, body(): pl.pallas_call(functools.partial(kernel, dims), out_shape=pltpu.VMEM((row...  31.1 us

profile of v5, /device:TPU:0, one launch (start us, length us, event | category | flops | bytes accessed | tf_op | source)
XLA Modules:
  0.0 31.7 jit_solution(13554704105429995709)
XLA Ops:
  0.0 31.1 %attention_step.1 = bf16[16,1024]{1,0:T(8,128)(2,1)S(1)} custom-call(bf16[16,1024]{1,0:T(8,128)(2,1)} %frames_hbm.1, bf16[32,128]{1,0:T(8,128)(2,1)} %bitcast.6, s32[1,128]{1,0:T(1,128)} %bitcast.7, s32[1,128]{1,0:T(1,128)} %bitcast.8, s32[1,128]{1,0:T(1,128)} %bitcast.9, bf16[3,4096,512]{2,1,0:T(8,128)(2,1)} %wqkv_hbm.1, bf16[512,4096]{1,0:T(8,128)(2,1)} %wout_hbm.1, ...), custom_call_target="tpu_custom_call" | custom-call | tf_op jit(solution)/shard_map/attention_step/pallas_call | solution.py:325
  31.1 0.6 %copy.10 = bf16[16,1024]{1,0:T(8,128)(2,1)} copy(bf16[16,1024]{1,0:T(8,128)(2,1)S(1)} %attention_step.1) | data formatting | bytes 65536
